TPU v7x, 512 devices: a whole 4x4x16 slice. The times are simulated.
512 devices in a mesh: doc: 64 (over y, z), bin: 8 (over x, core).
Axes of the slice: x: 4, y: 4, z: 16, core: 2. Of those that a mesh axis runs over, the one named last changes fastest.
Arguments:
- profiles: float32 [8192, 8192], P('doc', 'bin'), may hold values from -6 to 6
- assign: int32 [8192], P('doc'), may hold values from 0 to 4095, as said below
Outputs:
- centroids: float32 [8, 512, 8192], P('bin', 'doc')
- scores: float32 [4096, 8192], P('bin', 'doc')
Inputs may be any that keep to these rules, and one draw needn't show every extreme that they name: `assign`: cluster k belongs to owner (k % 512) // 8. In each aligned block of 128 documents, at most 8 documents are assigned to the clusters of one owner, and some owner has exactly 8 of them.
All inputs are finite; a program needn't handle non-finite values.
Results may differ from a plain program's by a relative error of at most 0.0029.
Values may be sent and summed in bfloat16 or wider, within the bound.
A program may use at most 64 MiB of HBM per device.

v0:
```python
import jax
import jax.numpy as jnp
from jax import lax
from jax.sharding import PartitionSpec as P

K = 4096


norm_epsilon = 1e-06


def shards(profiles, assign):
    doc_devs = lax.axis_size("doc")
    bin_devs = lax.axis_size("bin")
    doc_count, slab_width = profiles.shape
    slice_width = K // bin_devs
    part_width = slice_width // doc_devs
    owned_count = part_width * bin_devs
    capacity = 4 * doc_count // doc_devs
    owner_rank = assign % slice_width // part_width
    local_index = assign // slice_width * part_width + assign % part_width
    owner_hits = (owner_rank[:, None] == jnp.arange(doc_devs, dtype=jnp.int32)[None, :]).astype(
        jnp.int32
    )
    slot_rank = jnp.sum(jnp.cumsum(owner_hits, axis=0) * owner_hits, axis=1) - 1
    slot_index = owner_rank * capacity + slot_rank
    send_rows = (
        jnp.zeros((doc_devs * capacity, slab_width), jnp.float32).at[slot_index].set(profiles)
    )
    send_ids = jnp.full((doc_devs * capacity,), -1, jnp.int32).at[slot_index].set(local_index)
    send_rows = send_rows.reshape(doc_devs, capacity, slab_width)
    send_ids = send_ids.reshape(doc_devs, capacity)
    got_rows, got_ids = (
        lax.all_to_all(send_rows, "doc", split_axis=0, concat_axis=0, tiled=True),
        lax.all_to_all(send_ids, "doc", split_axis=0, concat_axis=0, tiled=True),
    )
    member = (
        got_ids.reshape(-1)[None, :] == jnp.arange(owned_count, dtype=jnp.int32)[:, None]
    ).astype(jnp.float32)
    cluster_sums = jnp.dot(
        member,
        got_rows.reshape(-1, slab_width),
        precision=lax.Precision.HIGHEST,
        preferred_element_type=jnp.float32,
    )
    cluster_sums = cluster_sums.reshape(bin_devs, part_width, slab_width)
    partial_squares = jnp.sum(cluster_sums * cluster_sums, axis=2)
    total_squares = lax.psum(partial_squares, "bin")
    unit = cluster_sums * lax.rsqrt(total_squares + norm_epsilon)[:, :, None]
    centroids = lax.all_to_all(unit, "bin", split_axis=0, concat_axis=2, tiled=True)
    gathered = lax.all_gather(unit.astype(jnp.bfloat16), "doc", axis=1, tiled=True)
    panel_rows = gathered.reshape(-1, slab_width)
    doc_values = profiles.astype(jnp.bfloat16)
    scores = lax.psum_scatter(
        lax.dot_general(
            panel_rows, doc_values, (((1,), (1,)), ((), ())), preferred_element_type=jnp.float32
        ),
        "bin",
        scatter_dimension=0,
        tiled=True,
    )
    return (centroids, scores)


def solution(mesh):
    in_specs = (P("doc", "bin"), P("doc"))
    out_specs = (P("bin", "doc", None), P("bin", "doc"))
    return jax.shard_map(shards, mesh=mesh, in_specs=in_specs, out_specs=out_specs, check_vma=False)
```

profile of v0, /device:TPU:1, one launch (start us, length us, event | category | flops | bytes accessed | tf_op | source)
XLA Modules:
  0.0 359.3 jit_solution(9232095160435295296)
XLA Ops:
  7.2 0.7 fusion.12
  7.8 0.1 fusion.9
  7.9 0.2 reduce_window_sum.11
  8.1 0.2 select_reduce_fusion
  8.3 1.0 scatter_custom_fusion
  9.3 0.7 all_to_all.22
  10.0 19.3 %all-to-all-start = ((s32[64,1,8]{2,1,0:T(1,128)}), s32[64,1,8]{2,1,0:T(1,128)S(1)}, u32[]{:S(2)}, u32[]{:S(2)}) async-start(s32[64,1,8]{2,1,0:T(1,128)} %bitcast), calls=%async_computation | async-start | bytes 65536 | tf_op jit(solution)/shard_map/all_to_all | solution.py:35
  29.3 3.0 scatter_custom_fusion.1
  32.2 10.3 %all-to-all-done = s32[64,1,8]{2,1,0:T(1,128)S(1)} async-done(((s32[64,1,8]{2,1,0:T(1,128)}), s32[64,1,8]{2,1,0:T(1,128)S(1)}, u32[]{:S(2)}, u32[]{:S(2)}) %all-to-all-start) | async-done | bytes 2080 | tf_op jit(solution)/shard_map/all_to_all | solution.py:35
  42.5 4.7 %all-to-all-start.1 = ((f32[64,8,1024]{2,1,0:T(8,128)}), f32[64,8,1024]{2,1,0:T(8,128)S(1)}, u32[]{:S(2)}, u32[]{:S(2)}) async-start(f32[64,8,1024]{2,1,0:T(8,128)} %bitcast.1), calls=%async_computation.1 | async-start | bytes 4194304 | tf_op jit(solution)/shard_map/all_to_all | solution.py:34
  47.2 0.0 copy-start
  47.2 0.0 all-gather.2.cloned.1.call-start
  47.3 0.5 broadcast.71
  47.8 0.7 reduce.3
  48.5 0.1 eq.45
  48.6 89.5 %all-to-all-done.1 = f32[64,8,1024]{2,1,0:T(8,128)S(1)} async-done(((f32[64,8,1024]{2,1,0:T(8,128)}), f32[64,8,1024]{2,1,0:T(8,128)S(1)}, u32[]{:S(2)}, u32[]{:S(2)}) %all-to-all-start.1) | async-done | bytes 2097184 | tf_op jit(solution)/shard_map/all_to_all | solution.py:34
  138.1 1.0 multiply_reduce_fusion
  139.1 20.0 %psum.7 = f32[8,8]{1,0:T(8,128)S(1)} all-reduce(f32[8,8]{1,0:T(8,128)S(1)} %get-tuple-element.6), channel_id=1, replica_groups=mesh['doc'=64,'bin'=8] {'bin'}, use_global_device_ids=true, to_apply=%region_5.6 | all-reduce | flops 64 | bytes 512 | tf_op jit(solution)/shard_map/psum | solution.py:48
  159.2 0.8 fusion.13
  159.9 0.0 all-gather.2.cloned.1.call-update
  160.0 0.0 reduce-scatter.2.cloned.1.call-start
  160.0 142.3 %all-gather.2.cloned.1.call-done = bf16[8,512,1024]{2,1,0:T(8,128)(2,1)} async-done(((bf16[8,8,1024]{2,1,0:T(8,128)(2,1)}), bf16[8,512,1024]{2,1,0:T(8,128)(2,1)}) %all-gather.2.cloned.1.call-update) | async-done | bytes 8388624 | tf_op jit(solution)/shard_map/all_gather | solution.py:51
  302.3 0.0 copy-done
  302.3 7.1 %fusion.4 = f32[4096,128]{1,0:T(8,128)} fusion(bf16[4096,1024]{1,0:T(8,128)(2,1)} %bitcast.18, f32[128,1024]{1,0:T(8,128)S(1)} %copy-done), kind=kOutput, calls=%fused_computation.6 | convolution fusion | flops 1073872896 | bytes 11010048 | tf_op jit(solution)/shard_map/dot_general | solution.py:55
  309.4 0.0 reduce-scatter.2.cloned.1.call-update
  309.5 19.1 %all_to_all.32 = f32[8,8,1024]{2,1,0:T(8,128)S(1)} all-to-all(f32[8,8,1024]{2,1,0:T(8,128)S(1)} %get-tuple-element.3), channel_id=1, replica_groups=mesh['doc'=64,'bin'=8] {'bin'}, dimensions={0} | all-to-all | bytes 524288 | tf_op jit(solution)/shard_map/all_to_all | solution.py:50
  328.6 23.1 %reduce-scatter.2.cloned.1.call-done = f32[512,128]{1,0:T(8,128)} async-done(((f32[4096,128]{1,0:T(8,128)}), f32[512,128]{1,0:T(8,128)}) %reduce-scatter.2.cloned.1.call-update) | async-done | bytes 262160 | tf_op jit(solution)/shard_map/reduce_scatter | solution.py:54
  351.8 0.7 copy.6
  (3 shorter events, 0.0 us)
Async XLA Ops:
  10.0 32.5 %all-to-all-start = ((s32[64,1,8]{2,1,0:T(1,128)}), s32[64,1,8]{2,1,0:T(1,128)S(1)}, u32[]{:S(2)}, u32[]{:S(2)}) async-start(s32[64,1,8]{2,1,0:T(1,128)} %bitcast), calls=%async_computation | async-start | bytes 65536 | tf_op jit(solution)/shard_map/all_to_all | solution.py:35
  42.5 95.6 %all-to-all-start.1 = ((f32[64,8,1024]{2,1,0:T(8,128)}), f32[64,8,1024]{2,1,0:T(8,128)S(1)}, u32[]{:S(2)}, u32[]{:S(2)}) async-start(f32[64,8,1024]{2,1,0:T(8,128)} %bitcast.1), calls=%async_computation.1 | async-start | bytes 4194304 | tf_op jit(solution)/shard_map/all_to_all | solution.py:34
  47.2 255.1 %copy-start = (f32[128,1024]{1,0:T(8,128)S(1)}, f32[128,1024]{1,0:T(8,128)}, u32[]{:S(2)}) copy-start(f32[128,1024]{1,0:T(8,128)} %param.2) | copy-start | bytes 1572868
  47.2 255.1 %all-gather.2.cloned.1.call-start = ((), (), s32[]{:S(2)}) async-start(), calls=%async_computation.4 | async-start | bytes 8519680 | tf_op jit(solution)/shard_map/all_gather | solution.py:51
  160.0 191.8 %reduce-scatter.2.cloned.1.call-start = ((), (), s32[]{:S(2)}) async-start(), calls=%async_computation.5 | async-start | bytes 2359296 | tf_op jit(solution)/shard_map/reduce_scatter | solution.py:54
Sparse Core Ops, SparseCore 0:
  160.1 142.1 all-gather.1
  309.6 42.1 reduce-scatter.1
where the time goes:
time: 361 us; the launch traced here: 359 us
  waiting for transfers between devices  265 us (73%)
  blocking collectives  39.2 us (11%)
  starting transfers between devices  24.1 us (7%)
  between operations  14.1 us (4%)
  matrix products  8.15 us (2%)
  local copies, waits for them, and re-layouts  5.95 us (2%)
    all_gather x1, waiting for transfers between devices, shards(): lax.all_gather(unit.astype(jnp.bfloat16), 'doc', axis=1, tiled=True)  142 us
    all_to_all x1, waiting for transfers between devices, shards(): lax.all_to_all(send_rows, 'doc', split_axis=0, concat_axis=0, tiled=True)  89.5 us
    reduce_scatter x1, waiting for transfers between devices, shards(): lax.psum_scatter(lax.dot_general(panel_rows, doc_values, (((1,), (1,)), (...  23.1 us
    psum x1, blocking collectives, shards(): total_squares = lax.psum(partial_squares, 'bin')  20 us
    all_to_all x1, starting transfers between devices, shards(): lax.all_to_all(send_ids, 'doc', split_axis=0, concat_axis=0, tiled=True)  19.3 us
    all_to_all x1, blocking collectives, shards(): lax.all_to_all(unit, 'bin', split_axis=0, concat_axis=2, tiled=True)  19.1 us
    all_to_all x1, waiting for transfers between devices, shards(): lax.all_to_all(send_ids, 'doc', split_axis=0, concat_axis=0, tiled=True)  10.3 us
  transfers between devices with their start and end apart: 4, of which 4 were waited for; matrix products, arithmetic and copies ran while one was open for 1% of the time, Pallas kernels for 0%

commit v1 on v0

v1 whole, which is shorter than its diff:
```python
import functools

import jax
import jax.numpy as jnp
from jax import lax
from jax.experimental import pallas as pl
from jax.experimental.pallas import tpu as pltpu
from jax.sharding import PartitionSpec as P

MESH = pl.DeviceIdType.MESH
EPS = 1e-06
K = 4096
DEPTH = 16
CHUNKS = 4
F32 = jnp.float32
LOW = jnp.bfloat16
NT = (((1,), (1,)), ((), ()))


def iota(shape, dim):
    return lax.broadcasted_iota(jnp.int32, shape, dim)


def kernel(
    Y, Z, B, p_ref, a_ref, cent_ref, score_ref,
    docs, own, ids, part, got, acc, sums, sum_out, sum_in, slab, sq_out, sq_in,
    nrm, fold_out, fold_in, unit,
    zr_send, zr_recv, zl_send, zl_recv, id_send, id_recv, own_send, own_recv,
    rs_send, rs_recv, sum_send, sum_recv, sq_send, sq_recv, nrm_send, nrm_recv,
    f_send, f_recv, u_send, u_recv,
):
    R, W = p_ref.shape
    NP = Z // 2
    PLANE = Y * B
    GROUP = K // B
    PART = GROUP // (Y * Z)
    OWN = PART * B
    LANES = PART * Z
    CR = R // CHUNKS
    SUB = R // B
    NC = Y * SUB
    doc, b = lax.axis_index("doc"), lax.axis_index("bin")
    y, z = doc // Z, doc % Z
    me = y * B + b

    def at_z(q):
        return (y * Z + lax.rem(z + q + Z, Z), b)

    def at_plane(idx):
        return ((idx // B) * Z + z, lax.rem(idx, B))

    def remote(src, dst, send, recv, device):
        return pltpu.make_async_remote_copy(
            src_ref=src, dst_ref=dst, send_sem=send, recv_sem=recv, device_id=device, device_id_type=MESH
        )

    def wait_bytes(ref, sem):
        pltpu.make_async_copy(ref, ref, sem).wait()

    barrier = pltpu.get_barrier_semaphore()

    @pl.loop(1, Z)
    def _(q):
        pl.semaphore_signal(barrier, inc=1, device_id=at_z(q), device_id_type=MESH)

    @pl.loop(1, PLANE)
    def _(q):
        pl.semaphore_signal(barrier, inc=1, device_id=at_plane(lax.rem(me + q, PLANE)), device_id_type=MESH)

    low = p_ref[...].astype(LOW)
    docs[0, 0:R, :] = low
    own[y] = low
    mine = jnp.broadcast_to(a_ref[...], (8, R))
    ids[0, :, 0:R] = mine
    pl.semaphore_wait(barrier, Z + PLANE - 2)

    def right(s, to, row, c):
        return remote(docs.at[s, pl.ds(c * CR, CR)], docs.at[to, pl.ds(row + c * CR, CR)],
                      zr_send.at[s, c], zr_recv.at[to, c], at_z(1))

    def left(s, row, to, c):
        return remote(docs.at[s, pl.ds(row + c * CR, CR)], docs.at[to, pl.ds(R + c * CR, CR)],
                      zl_send.at[s, c], zl_recv.at[to, c], at_z(-1))

    for c in range(CHUNKS):
        right(0, 1, 0, c).start()
        left(0, 0, 1, c).start()
    id_copies = []
    for q in range(1, Z):
        pair, half = (q % NP, int(q == NP)) if q <= NP else (Z - q, 1)
        id_copies.append(remote(
            ids.at[0, :, pl.ds(0, R)], ids.at[pair, :, pl.ds(half * R, R)],
            id_send.at[q], id_recv.at[q], at_z(q)))
        id_copies[-1].start()
    own_copies = []
    for q in range(1, Y):
        own_copies.append(remote(
            docs.at[0, pl.ds(0, R)], own.at[y], own_send.at[q], own_recv.at[q],
            (lax.rem(y + q, Y) * Z + z, b)))
        own_copies[-1].start()
    acc[...] = jnp.zeros_like(acc)
    sums[...] = jnp.zeros_like(sums)

    def partial(p):
        for v in range(Y):
            g = lax.dot_general(own[v], docs[p], NT, preferred_element_type=F32)
            part[p, :, v * SUB:(v + 1) * SUB, :] = g.reshape(B, SUB, 2 * R).astype(part.dtype)
        for q in range(1, B):
            to = lax.rem(b + q, B)
            remote(part.at[p, to], got.at[p, q - 1], rs_send.at[p], rs_recv.at[p], (doc, to)).start()

    def add_sums(p):
        a = ids[p, 0:1, :]
        rank = (a & (GROUP - 1)) // PART
        row = (rank // Z) * OWN + (a // GROUP) * PART + (a & (PART - 1))
        row = jnp.where((rank & (Z - 1)) == z, row, -1)
        hot = (iota((Y * OWN, 2 * R), 0) == row).astype(F32).astype(LOW)
        sums[...] += jnp.dot(hot, docs[p], preferred_element_type=F32)

    def fold(p, first, count):
        h = part[p, b].astype(F32)
        for i in range(B - 1):
            h += got[p, i].astype(F32)
        hi = h.astype(LOW)
        lo = (h - hi.astype(F32)).astype(LOW)
        both = jnp.concatenate([hi, lo], axis=0)
        col = jnp.transpose(jnp.broadcast_to(ids[p, 0:1, :], (128, 2 * R)))
        for g in range(first, first + count):
            hot = jnp.concatenate(
                [(col == iota((2 * R, 128), 1) + (g * GROUP + t * 128)).astype(F32).astype(LOW)
                 for t in range(GROUP // 128)], axis=1)
            d = jnp.dot(both, hot, preferred_element_type=F32)
            acc[:, g * GROUP:(g + 1) * GROUP] += d[0:NC] + d[NC:]

    def sum_copy(q):
        v = lax.rem(y + q, Y)
        return remote(sum_out.at[v], sum_in.at[q - 1], sum_send.at[q - 1], sum_recv.at[q - 1], (v * Z + z, b))

    @pl.loop(1, NP + 3)
    def _(s):
        for c in range(CHUNKS):
            early = c < CHUNKS // 2

            @pl.when(s < NP)
            def _():
                right(0, s, 0, c).wait_recv()
                go = lambda: right(s, lax.rem(s + 1, NP), jnp.where(s == NP - 1, R, 0), c).start()
                go() if early else pl.when(s < NP - 1)(go)
                left(0, 0, s, c).wait_recv()
                go_left = lambda: left(s, R, lax.rem(s + 1, NP), c).start()
                pl.when(s < NP - 1)(go_left) if early else go_left()

            @pl.when(s == NP)
            def _():
                if early:
                    right(0, 0, R, c).wait_recv()
                else:
                    left(0, 0, 0, c).wait_recv()

            if c == 0:

                @pl.when(s == 2)
                def _():
                    for copy in id_copies:
                        copy.wait()
                    for q in range(1, Y):
                        own_copies[q - 1].wait_send()
                        from_y = lax.rem(y - q + Y, Y)
                        remote(own.at[0], own.at[from_y], own_send.at[q], own_recv.at[q], (doc, b)).wait_recv()

                pl.when((s >= 2) & (s < NP + 1))(lambda: partial(s - 1))
            if c == 1:
                pl.when((s >= 2) & (s < NP + 1))(lambda: add_sums(s - 1))
            if c == 2:

                @pl.when(s == NP + 1)
                def _():
                    add_sums(0)
                    for v in range(Y):
                        sum_out[v] = sums[v * OWN:(v + 1) * OWN, :].astype(LOW)
                    for q in range(1, Y):
                        sum_copy(q).start()
                    partial(0)

            if c >= 2:

                @pl.when(s >= 3)
                def _():
                    p = lax.rem(s - 2, NP)
                    if c == 2:
                        wait_bytes(got.at[p], rs_recv.at[p])
                    half = B // 2
                    fold(p, (c - 2) * half, half)

    for g in range(B):
        fold_out[g] = acc[:, g * GROUP:(g + 1) * GROUP].astype(LOW)

    def fold_piece(idx):
        v, g = idx // B, lax.rem(idx, B)
        return (fold_out.at[g, pl.ds(pl.multiple_of(v * SUB, SUB), SUB)],
                fold_in.at[me])

    @pl.loop(1, PLANE)
    def _(q):
        idx = lax.rem(me + q, PLANE)
        src, dst = fold_piece(idx)
        remote(src, dst, f_send, f_recv, at_plane(idx)).start()

    src, dst = fold_piece(me)
    pltpu.make_async_copy(src, dst, f_recv).start()

    for q in range(1, Y):
        sum_copy(q).wait()
    total = sums[pl.ds(pl.multiple_of(y * OWN, OWN), OWN), :]
    for q in range(Y - 1):
        total += sum_in[q].astype(F32)
    slab[...] = total
    square = jnp.sum(total * total, axis=1, keepdims=True)
    square = jnp.broadcast_to(square, (OWN, 128))
    if OWN < 128:
        square = jnp.concatenate([square, jnp.zeros((128 - OWN, 128), F32)], axis=0)
    square = jnp.transpose(square)[0:8]
    sq_out[...] = square

    @pl.loop(1, PLANE)
    def _(q):
        idx = lax.rem(me + q, PLANE)
        remote(sq_out, sq_in.at[PLANE - 1 - q], sq_send, sq_recv, at_plane(idx)).start()

    wait_bytes(sq_in, sq_recv)
    sub = iota((8, 128), 0)
    lane = iota((8, 128), 1)
    table = jnp.zeros((8, 128), F32)
    for i in range(PLANE):
        row = sq_out[...] if i == PLANE - 1 else sq_in[i]
        v = lax.rem(me + i + 1, PLANE) // B
        table += jnp.where(sub == v, row, 0.0)
    inverse = lax.rsqrt(table + EPS)
    ours = jnp.sum(jnp.where(sub == y, inverse, 0.0), axis=0, keepdims=True)
    turned = pltpu.roll(inverse, lax.rem((z - b) * PART + 128, 128), 1)
    turned = jnp.where((lane >= z * PART) & (lane < (z + 1) * PART), turned, 0.0)
    nrm[Z - 1] = turned

    @pl.loop(1, Z)
    def _(q):
        remote(nrm.at[Z - 1], nrm.at[Z - 1 - q], nrm_send, nrm_recv, at_z(q)).start()

    scale = jnp.transpose(jnp.broadcast_to(ours, (128, 128)))[0:OWN]
    for t in range(W // 128):
        unit[:, t * 128:(t + 1) * 128] = slab[:, t * 128:(t + 1) * 128] * scale
    for q in range(1, B):
        to = lax.rem(b + q, B)
        remote(unit.at[pl.ds(pl.multiple_of(to * PART, PART), PART)],
               cent_ref.at[0, :, pl.ds(pl.multiple_of(b * W, W), W)],
               u_send, u_recv, (doc, to)).start()
    cent_ref[0, :, pl.ds(pl.multiple_of(b * W, W), W)] = unit[pl.ds(pl.multiple_of(b * PART, PART), PART), :]

    wait_bytes(fold_in, f_recv)
    raw = fold_in[0:B].astype(F32)
    for v in range(1, Y):
        raw += fold_in[v * B:(v + 1) * B].astype(F32)
    raw = raw.reshape(R, GROUP)
    wait_bytes(nrm.at[pl.ds(0, Z - 1)], nrm_recv)
    rows = nrm[0]
    for i in range(1, Z):
        rows += nrm[i]
    for v in range(Y):
        tile = raw[:, v * LANES:(v + 1) * LANES] * rows[v:v + 1, :]
        score_ref[v * LANES:(v + 1) * LANES, :] = jnp.transpose(tile)

    @pl.loop(0, NP)
    def _(s):
        for c in range(CHUNKS):
            early = c < CHUNKS // 2
            wait_right = lambda: right(s, s, 0, c).wait_send()
            wait_left = lambda: left(s, 0, s, c).wait_send()
            wait_right() if early else pl.when(s < NP - 1)(wait_right)
            pl.when(s < NP - 1)(wait_left) if early else wait_left()
        wait_bytes(part.at[s, pl.ds(0, B - 1)], rs_send.at[s])

    wait_bytes(fold_in.at[pl.ds(0, PLANE - 1)], f_send)
    wait_bytes(sq_in, sq_send)
    wait_bytes(nrm.at[pl.ds(0, Z - 1)], nrm_send)
    wait_bytes(cent_ref.at[0, :, pl.ds(0, (B - 1) * W)], u_send)
    wait_bytes(cent_ref.at[0, :, pl.ds(0, (B - 1) * W)], u_recv)


def program(mesh, depth, clusters):
    B = mesh.shape["bin"]
    Z = depth
    Y = mesh.shape["doc"] // Z
    NP = Z // 2
    global K
    K = clusters

    def shards(profiles, assign):
        R, W = profiles.shape
        group = clusters // B
        own = group // (Y * Z) * B
        SUB = R // B
        NC = Y * SUB
        plane = Y * B
        dma = pltpu.SemaphoreType.DMA
        scratch = [
            pltpu.VMEM((NP, 2 * R, W), LOW),
            pltpu.VMEM((Y, R, W), LOW),
            pltpu.VMEM((NP, 8, 2 * R), jnp.int32),
            pltpu.VMEM((NP, B, NC, 2 * R), F32),
            pltpu.VMEM((NP, B - 1, NC, 2 * R), F32),
            pltpu.VMEM((NC, clusters), F32),
            pltpu.VMEM((Y * own, W), F32),
            pltpu.VMEM((Y, own, W), LOW),
            pltpu.VMEM((Y - 1, own, W), LOW),
            pltpu.VMEM((own, W), F32),
            pltpu.VMEM((8, 128), F32),
            pltpu.VMEM((plane - 1, 8, 128), F32),
            pltpu.VMEM((Z, 8, 128), F32),
            pltpu.VMEM((B, NC, group), LOW),
            pltpu.VMEM((plane, SUB, group), LOW),
            pltpu.VMEM((own, W), F32),
            *[dma((NP, CHUNKS))] * 4,
            *[dma((Z,))] * 2,
            *[dma((Y,))] * 2,
            *[dma((NP,))] * 2,
            *[dma((Y - 1,))] * 2,
            *[dma] * 8,
        ]
        return pl.pallas_call(
            functools.partial(kernel, Y, Z, B),
            out_shape=(
                jax.ShapeDtypeStruct((1, group // (Y * Z), B * W), F32),
                jax.ShapeDtypeStruct((group, R), F32),
            ),
            in_specs=[pl.BlockSpec(memory_space=pltpu.VMEM)] * 2,
            out_specs=(pl.BlockSpec(memory_space=pltpu.VMEM),) * 2,
            scratch_shapes=scratch,
            compiler_params=pltpu.CompilerParams(
                collective_id=0, has_side_effects=True, vmem_limit_bytes=40 * 2**20
            ),
        )(profiles, assign.reshape(1, -1))

    return jax.shard_map(
        shards,
        mesh=mesh,
        in_specs=(P("doc", "bin"), P("doc")),
        out_specs=(P("bin", "doc", None), P("bin", "doc")),
        check_vma=False,
    )


def solution(mesh):
    return program(mesh, DEPTH, 4096)
```

time: 361 us -> 106 us (0.29)
  waiting for transfers between devices: 265 us -> 0 us
  Pallas kernels: 0 us -> 102 us
  blocking collectives: 39.2 us -> 0 us
  starting transfers between devices: 24.1 us -> 0 us
  between operations: 14.1 us -> 0.65 us
  matrix products: 8.15 us -> 0 us
    all_gather x1 -> x0, waiting for transfers between devices: 142 us -> none  [shards(): lax.all_gather(unit.astype(jnp.bfloat16), 'doc', axis=1, tiled=True)]
    pallas_call x0 -> x1, Pallas kernels: none -> 102 us  [shards(): pl.pallas_call(functools.partial(kernel, Y, Z, B), out_shape=(jax.ShapeDt...]
    all_to_all x2 -> x0, waiting for transfers between devices: 99.8 us -> none  [the longest x1 89.5 us: shards(): lax.all_to_all(send_rows, 'doc', split_axis=0, concat_axis=0, tiled=True)]
    all_to_all x2 -> x0, starting transfers between devices: 24 us -> none  [the longest x1 19.3 us: shards(): lax.all_to_all(send_ids, 'doc', split_axis=0, concat_axis=0, tiled=True)]
    reduce_scatter x1 -> x0, waiting for transfers between devices: 23.1 us -> none  [shards(): lax.psum_scatter(lax.dot_general(panel_rows, doc_values, (((1,), (1,)), (...]
    psum x1 -> x0, blocking collectives: 20 us -> none  [shards(): total_squares = lax.psum(partial_squares, 'bin')]
    all_to_all x1 -> x0, blocking collectives: 19.1 us -> none  [shards(): lax.all_to_all(unit, 'bin', split_axis=0, concat_axis=2, tiled=True)]
    dot_general x2 -> x0, matrix products: 8.15 us -> none  [the longest x1 7.13 us: shards(): lax.dot_general(panel_rows, doc_values, (((1,), (1,)), ((), ())), preferr...]
  transfers between devices with their start and end apart: 4 -> 0, of which waited for: 4 -> 0; matrix products, arithmetic and copies ran while one was open for 1% -> 0% of each run, Pallas kernels for 0% -> 0%
where the time goes in v1:
time: 106 us
  Pallas kernels  102 us (96%)
  local copies, waits for them, and re-layouts  3.1 us (3%)
    pallas_call x1, Pallas kernels, shards(): pl.pallas_call(functools.partial(kernel, Y, Z, B), out_shape=(jax.ShapeDt...  102 us
    unnamed x6, local copies, waits for them, and re-layouts  3.1 us

profile of v1, /device:TPU:1, one launch (start us, length us, event | category | flops | bytes accessed | tf_op | source)
XLA Modules:
  0.0 105.7 jit_solution(1908306034120599716)
XLA Ops:
  0.6 0.0 copy-start.1
  0.6 0.6 copy-done.1
  1.3 0.0 copy-start
  1.3 1.0 copy-done
  2.3 101.9 %shard_map.41 = (f32[1,8,8192]{2,1,0:T(8,128)S(1)}, f32[512,128]{1,0:T(8,128)S(1)}) custom-call(f32[128,1024]{1,0:T(8,128)S(1)} %copy-done, s32[1,128]{1,0:T(1,128)S(1)} %bitcast.1), custom_call_target="tpu_custom_call" | custom-call | tf_op jit(solution)/shard_map/pallas_call | solution.py:328
  104.3 0.7 copy.6
  105.0 0.7 copy.7
Async XLA Ops:
  0.6 0.7 copy-start.1
  1.3 1.0 copy-start

commit v2 on v1

v2 whole, which is shorter than its diff:
```python
import functools

import jax
import jax.numpy as jnp
from jax import lax
from jax.experimental import pallas as pl
from jax.experimental.pallas import tpu as pltpu
from jax.sharding import PartitionSpec as P

MESH = pl.DeviceIdType.MESH
EPS = 1e-06
DEPTH = 16
CHUNKS = 4
F32 = jnp.float32
LOW = jnp.bfloat16
NT = (((1,), (1,)), ((), ()))


def iota(shape, dim):
    return lax.broadcasted_iota(jnp.int32, shape, dim)


def kernel(
    Y, Z, B, K, p_hbm, a_hbm, cent_ref, score_ref,
    p_ref, a_ref, docs, own, ids, col, part, got, part0, got0, part_pen, got_pen, part_last, got_last,
    acc, sums, pay_out, pay_in, sq_out, sq_in, nrm, fold_out, fold_in, cent_raw, colscale,
    in_sem, zr_send, zr_recv, zl_send, zl_recv, id_send, id_recv, own_send, own_recv,
    rs_send, rs_recv, pay_send, pay_recv, sq_send, sq_recv, nrm_send, nrm_recv,
    f_send, f_recv, u_send, u_recv,
):
    R, W = p_ref.shape
    NP = Z // 2
    LAST = NP
    PLANE = Y * B
    GROUP = K // B
    PART = GROUP // (Y * Z)
    OWN = PART * B
    LANES = PART * Z
    CR = R // CHUNKS
    SUB = R // B
    NC = Y * SUB
    CAP = 8
    doc, b = lax.axis_index("doc"), lax.axis_index("bin")
    y, z = doc // Z, doc % Z
    me = y * B + b

    def at_z(q):
        return (y * Z + lax.rem(z + q + Z, Z), b)

    def at_y(q):
        return (lax.rem(y + q, Y) * Z + z, b)

    def at_plane(idx):
        return ((idx // B) * Z + z, lax.rem(idx, B))

    def remote(src, dst, send, recv, device):
        return pltpu.make_async_remote_copy(
            src_ref=src, dst_ref=dst, send_sem=send, recv_sem=recv, device_id=device, device_id_type=MESH
        )

    def wait_bytes(ref, sem):
        pltpu.make_async_copy(ref, ref, sem).wait()

    fetch = pltpu.make_async_copy(p_hbm, p_ref, in_sem.at[0])
    fetch.start()
    fetch_ids = pltpu.make_async_copy(a_hbm, a_ref, in_sem.at[1])
    fetch_ids.start()

    barrier = pltpu.get_barrier_semaphore()

    @pl.loop(1, Z)
    def _(q):
        pl.semaphore_signal(barrier, inc=1, device_id=at_z(q), device_id_type=MESH)

    @pl.loop(1, PLANE)
    def _(q):
        pl.semaphore_signal(barrier, inc=1, device_id=at_plane(lax.rem(me + q, PLANE)), device_id_type=MESH)

    fetch.wait()
    fetch_ids.wait()
    low = p_ref[...].astype(LOW)
    docs[0, 0:R, :] = low
    own[y] = low
    ids[0, :, 0:R] = jnp.broadcast_to(a_ref[...], (8, R))
    pl.semaphore_wait(barrier, Z + PLANE - 2)

    def right(s, to, row, c):
        return remote(docs.at[s, pl.ds(c * CR, CR)], docs.at[to, pl.ds(row + c * CR, CR)],
                      zr_send.at[s, c], zr_recv.at[to, c], at_z(1))

    def left(s, row, to, c):
        return remote(docs.at[s, pl.ds(row + c * CR, CR)], docs.at[to, pl.ds(R + c * CR, CR)],
                      zl_send.at[s, c], zl_recv.at[to, c], at_z(-1))

    for c in range(CHUNKS):
        right(0, 1, 0, c).start()
        left(0, 0, 1, c).start()
    id_copies = []
    for q in range(1, Z):
        pair, half = (q % NP, int(q == NP)) if q <= NP else (Z - q, 1)
        id_copies.append(remote(
            ids.at[0, :, pl.ds(0, R)], ids.at[pair, :, pl.ds(half * R, R)],
            id_send.at[q], id_recv.at[q], at_z(q)))
        id_copies[-1].start()
    own_copies = []
    for q in range(1, Y):
        own_copies.append(remote(docs.at[0, pl.ds(0, R)], own.at[y], own_send.at[q], own_recv.at[q], at_y(q)))
        own_copies[-1].start()
    acc[...] = jnp.zeros_like(acc)
    sums[...] = jnp.zeros_like(sums)

    def partial(rows, unit, out, into):
        n = rows.shape[0]
        for v in range(Y):
            g = lax.dot_general(own[v], rows, NT, preferred_element_type=F32)
            out[:, v * SUB:(v + 1) * SUB, :] = g.reshape(B, SUB, n).astype(out.dtype)
        for q in range(1, B):
            to = lax.rem(b + q, B)
            remote(out.at[to], into.at[q - 1], rs_send.at[unit], rs_recv.at[unit], (doc, to)).start()

    def place(rows, a, column, unit):
        n = rows.shape[0]
        a = jnp.broadcast_to(a, (16, n))
        sub = iota((16, n), 0)
        lane = iota((16, n), 1)
        owner = jnp.where(sub < Y, lax.rem(y + sub, Y) * Z + z, -1)
        match = ((a & (GROUP - 1)) // PART) == owner
        local = (a // GROUP) * PART + (a & (PART - 1))
        earlier = (iota((n, n), 0) < iota((n, n), 1)) & (iota((n, n), 0) // R == iota((n, n), 1) // R)
        before = jnp.dot(match.astype(F32).astype(LOW), earlier.astype(F32).astype(LOW), preferred_element_type=F32)
        slot = jnp.where(match, before + CAP * (lane // R).astype(F32), -1.0)
        number = sub.astype(F32)
        pick = jnp.concatenate(
            [(number == slot[q:q + 1]).astype(F32).astype(LOW) for q in range(1, Y)], axis=0)
        home = (column // GROUP) * PART + (column & (PART - 1))
        home = (home == iota((n, 128), 1)).astype(F32).astype(LOW)
        picked = jnp.dot(pick, rows, preferred_element_type=F32).astype(LOW)
        where = jnp.dot(pick, home, preferred_element_type=F32).astype(LOW)
        for q in range(1, Y):
            pay_out[unit, q - 1, :, 0:W] = picked[(q - 1) * 16:q * 16]
            pay_out[unit, q - 1, :, W:W + 128] = where[(q - 1) * 16:q * 16]
            remote(pay_out.at[unit, q - 1], pay_in.at[unit, q - 1], pay_send.at[unit], pay_recv.at[unit], at_y(q)).start()
        row = jnp.where(match[0:1], local[0:1], -1)
        hot = (iota((OWN, n), 0) == row).astype(F32).astype(LOW)
        sums[...] += jnp.dot(hot, rows, preferred_element_type=F32)

    def add_placed(unit):
        wait_bytes(pay_in.at[unit], pay_recv.at[unit])
        for q in range(1, Y):
            d = lax.dot_general(pay_in[unit, q - 1, :, W:W + 128], pay_in[unit, q - 1, :, 0:W],
                                (((0,), (0,)), ((), ())), preferred_element_type=F32)
            sums[...] += d[0:OWN]

    def fold(out, into, column, first, count):
        h = out[b].astype(F32)
        for i in range(B - 1):
            h += into[i].astype(F32)
        hi = h.astype(LOW)
        lo = (h - hi.astype(F32)).astype(LOW)
        both = jnp.concatenate([hi, lo], axis=0)
        n = h.shape[1]
        for g in range(first, first + count):
            hot = jnp.concatenate(
                [(column == iota((n, 128), 1) + (g * GROUP + t * 128)).astype(F32).astype(LOW)
                 for t in range(GROUP // 128)], axis=1)
            d = jnp.dot(both, hot, preferred_element_type=F32)
            acc[:, g * GROUP:(g + 1) * GROUP] += d[0:NC] + d[NC:]

    @pl.loop(1, NP)
    def _(s):
        for c in range(CHUNKS):
            early = c < CHUNKS // 2
            right(0, s, 0, c).wait_recv()
            go = lambda: right(s, lax.rem(s + 1, NP), jnp.where(s == NP - 1, R, 0), c).start()
            go() if early else pl.when(s < NP - 1)(go)
            left(0, 0, s, c).wait_recv()
            go_left = lambda: left(s, R, lax.rem(s + 1, NP), c).start()
            pl.when(s < NP - 1)(go_left) if early else go_left()

            if c == 0:

                @pl.when(s == 2)
                def _():
                    for copy in id_copies:
                        copy.wait()
                    for q in range(1, Y):
                        own_copies[q - 1].wait_send()
                        from_y = lax.rem(y - q + Y, Y)
                        remote(own.at[0], own.at[from_y], own_send.at[q], own_recv.at[q], (doc, b)).wait_recv()

                    @pl.loop(0, NP)
                    def _(p):
                        col[p] = jnp.transpose(jnp.broadcast_to(ids[p, 0:1, :], (128, 2 * R)))

                pl.when(s >= 2)(lambda: partial(docs[s - 1], s - 1, part.at[s - 2], got.at[s - 2]))

            if c == 1:
                pl.when(s >= 2)(lambda: place(docs[s - 1], ids[s - 1, 0:1, :], col[s - 1], s - 1))

                @pl.when(s == 2)
                def _():
                    place(docs[0, 0:R, :], ids[0, 0:1, 0:R], col[0, 0:R, :], 0)
                    partial(docs[0, 0:R, :], 0, part0, got0)

            if c >= 2:

                @pl.when(s >= 3)
                def _():
                    p = s - 2
                    if c == 2:
                        wait_bytes(got.at[p - 1], rs_recv.at[p])
                    half = B // 2
                    fold(part.at[p - 1], got.at[p - 1], col[p], (c - 2) * half, half)
                    if c == 3:
                        add_placed(p)

    place(docs[NP - 1], ids[NP - 1, 0:1, :], col[NP - 1], NP - 1)
    partial(docs[NP - 1], NP - 1, part_pen, got_pen)
    wait_bytes(got0, rs_recv.at[0])
    fold(part0, got0, col[0, 0:R, :], 0, B)
    add_placed(0)
    for c in range(CHUNKS // 2):
        right(0, 0, R, c).wait_recv()
        left(0, 0, 0, c + CHUNKS // 2).wait_recv()
    place(docs[0, R:2 * R, :], ids[0, 0:1, R:2 * R], col[0, R:2 * R, :], LAST)
    partial(docs[0, R:2 * R, :], LAST, part_last, got_last)
    wait_bytes(got.at[NP - 3], rs_recv.at[NP - 2])
    fold(part.at[NP - 3], got.at[NP - 3], col[NP - 2], 0, B)
    add_placed(NP - 2)
    add_placed(NP - 1)
    add_placed(LAST)

    def slab_copy(to):
        return remote(sums.at[pl.ds(pl.multiple_of(to * PART, PART), PART)],
                      cent_raw.at[:, pl.ds(pl.multiple_of(b * W, W), W)], u_send, u_recv, (doc, to))

    square = jnp.sum(sums[...] * sums[...], axis=1, keepdims=True)
    square = jnp.broadcast_to(square, (OWN, 128))
    if OWN < 128:
        square = jnp.concatenate([square, jnp.zeros((128 - OWN, 128), F32)], axis=0)
    sq_out[...] = jnp.transpose(square)[0:1]

    @pl.loop(1, PLANE)
    def _(q):
        idx = lax.rem(me + q, PLANE)
        remote(sq_out, sq_in.at[PLANE - 1 - q], sq_send, sq_recv, at_plane(idx)).start()

    for q in range(1, B):
        slab_copy(lax.rem(b + q, B)).start()
    cent_raw[:, pl.ds(pl.multiple_of(b * W, W), W)] = sums[pl.ds(pl.multiple_of(b * PART, PART), PART), :]

    wait_bytes(got_pen, rs_recv.at[NP - 1])
    fold(part_pen, got_pen, col[NP - 1], 0, B)
    wait_bytes(got_last, rs_recv.at[LAST])
    fold(part_last, got_last, col[0, R:2 * R, :], 0, B)

    for g in range(B):
        fold_out[g] = acc[:, g * GROUP:(g + 1) * GROUP].astype(LOW)

    def fold_piece(idx):
        v, g = idx // B, lax.rem(idx, B)
        return fold_out.at[g, pl.ds(pl.multiple_of(v * SUB, SUB), SUB)], fold_in.at[me]

    @pl.loop(1, PLANE)
    def _(q):
        idx = lax.rem(me + q, PLANE)
        src, dst = fold_piece(idx)
        remote(src, dst, f_send, f_recv, at_plane(idx)).start()

    src, dst = fold_piece(me)
    pltpu.make_async_copy(src, dst, f_recv).start()

    wait_bytes(sq_in, sq_recv)
    sub = iota((8, 128), 0)
    lane = iota((8, 128), 1)
    table = jnp.zeros((8, 128), F32)
    for i in range(PLANE):
        row = sq_out[...] if i == PLANE - 1 else sq_in[i]
        v = lax.rem(me + i + 1, PLANE) // B
        table += jnp.where(sub == v, row, 0.0)
    inverse = lax.rsqrt(table + EPS)
    turned = pltpu.roll(inverse, lax.rem((z - b) * PART + 128, 128), 1)
    turned = jnp.where((lane >= z * PART) & (lane < (z + 1) * PART), turned, 0.0)
    nrm[Z - 1] = turned[0:Y]

    @pl.loop(1, Z)
    def _(q):
        remote(nrm.at[Z - 1], nrm.at[Z - 1 - q], nrm_send, nrm_recv, at_z(q)).start()

    ours = jnp.sum(jnp.where(sub == y, inverse, 0.0), axis=0, keepdims=True)
    colscale[...] = jnp.transpose(jnp.broadcast_to(ours, (128, 128)))
    scale = colscale[pl.ds(pl.multiple_of(b * PART, PART), PART), :]
    wait_bytes(cent_raw.at[:, pl.ds(0, (B - 1) * W)], u_recv)
    for t in range(B * W // 128):
        cent_ref[0, :, t * 128:(t + 1) * 128] = cent_raw[:, t * 128:(t + 1) * 128] * scale

    wait_bytes(fold_in, f_recv)
    raw = fold_in[0:B].astype(F32)
    for v in range(1, Y):
        raw += fold_in[v * B:(v + 1) * B].astype(F32)
    raw = raw.reshape(R, GROUP)
    wait_bytes(nrm.at[pl.ds(0, Z - 1)], nrm_recv)
    rows = nrm[0]
    for i in range(1, Z):
        rows += nrm[i]
    for v in range(Y):
        tile = raw[:, v * LANES:(v + 1) * LANES] * rows[v:v + 1, :]
        score_ref[v * LANES:(v + 1) * LANES, :] = jnp.transpose(tile)

    @pl.loop(0, NP)
    def _(s):
        for c in range(CHUNKS):
            early = c < CHUNKS // 2
            wait_right = lambda: right(s, s, 0, c).wait_send()
            wait_left = lambda: left(s, 0, s, c).wait_send()
            wait_right() if early else pl.when(s < NP - 1)(wait_right)
            pl.when(s < NP - 1)(wait_left) if early else wait_left()

    for p in range(NP - 2):
        wait_bytes(got.at[p], rs_send.at[p + 1])
    wait_bytes(got0, rs_send.at[0])
    wait_bytes(got_pen, rs_send.at[NP - 1])
    wait_bytes(got_last, rs_send.at[LAST])
    for u in range(NP + 1):
        wait_bytes(pay_in.at[u], pay_send.at[u])
    wait_bytes(fold_in.at[pl.ds(0, PLANE - 1)], f_send)
    wait_bytes(sq_in, sq_send)
    wait_bytes(nrm.at[pl.ds(0, Z - 1)], nrm_send)
    wait_bytes(cent_raw.at[:, pl.ds(0, (B - 1) * W)], u_send)


def program(mesh, Z, clusters):
    B = mesh.shape["bin"]
    Y = mesh.shape["doc"] // Z
    NP = Z // 2

    def shards(profiles, assign):
        R, W = profiles.shape
        group = clusters // B
        part = group // (Y * Z)
        own = part * B
        SUB = R // B
        NC = Y * SUB
        plane = Y * B
        dma = pltpu.SemaphoreType.DMA
        scratch = [
            pltpu.VMEM((R, W), F32),
            pltpu.VMEM((1, R), jnp.int32),
            pltpu.VMEM((NP, 2 * R, W), LOW),
            pltpu.VMEM((Y, R, W), LOW),
            pltpu.VMEM((NP, 8, 2 * R), jnp.int32),
            pltpu.VMEM((NP, 2 * R, 128), jnp.int32),
            pltpu.VMEM((NP - 2, B, NC, 2 * R), F32),
            pltpu.VMEM((NP - 2, B - 1, NC, 2 * R), F32),
            pltpu.VMEM((B, NC, R), F32),
            pltpu.VMEM((B - 1, NC, R), F32),
            pltpu.VMEM((B, NC, 2 * R), LOW),
            pltpu.VMEM((B - 1, NC, 2 * R), LOW),
            pltpu.VMEM((B, NC, R), LOW),
            pltpu.VMEM((B - 1, NC, R), LOW),
            pltpu.VMEM((NC, clusters), F32),
            pltpu.VMEM((own, W), F32),
            pltpu.VMEM((NP + 1, Y - 1, 16, W + 128), LOW),
            pltpu.VMEM((NP + 1, Y - 1, 16, W + 128), LOW),
            pltpu.VMEM((1, 128), F32),
            pltpu.VMEM((plane - 1, 1, 128), F32),
            pltpu.VMEM((Z, Y, 128), F32),
            pltpu.VMEM((B, NC, group), LOW),
            pltpu.VMEM((plane, SUB, group), LOW),
            pltpu.VMEM((part, B * W), F32),
            pltpu.VMEM((128, 128), F32),
            dma((2,)),
            *[dma((NP, CHUNKS))] * 4,
            *[dma((Z,))] * 2,
            *[dma((Y,))] * 2,
            *[dma((NP + 1,))] * 4,
            *[dma] * 8,
        ]
        return pl.pallas_call(
            functools.partial(kernel, Y, Z, B, clusters),
            out_shape=(
                jax.ShapeDtypeStruct((1, part, B * W), F32),
                jax.ShapeDtypeStruct((group, R), F32),
            ),
            in_specs=[pl.BlockSpec(memory_space=pltpu.HBM)] * 2,
            out_specs=(pl.BlockSpec(memory_space=pltpu.VMEM),) * 2,
            scratch_shapes=scratch,
            compiler_params=pltpu.CompilerParams(
                collective_id=0, has_side_effects=True, vmem_limit_bytes=48 * 2**20
            ),
        )(profiles, assign.reshape(1, -1))

    return jax.shard_map(
        shards,
        mesh=mesh,
        in_specs=(P("doc", "bin"), P("doc")),
        out_specs=(P("bin", "doc", None), P("bin", "doc")),
        check_vma=False,
    )


def solution(mesh):
    return program(mesh, DEPTH, 4096)
```

time: 106 us -> 92.2 us (0.87)
  Pallas kernels: 102 us -> 88.3 us
    pallas_call x1, Pallas kernels: 102 us -> 88.3 us  [shards(): pl.pallas_call(functools.partial(kernel, Y, Z, B, clusters), out_shape=(j...]
where the time goes in v2:
time: 92.2 us; the launch traced here: 92.1 us
  Pallas kernels  88.3 us (96%)
  local copies, waits for them, and re-layouts  3.1 us (3%)
    pallas_call x1, Pallas kernels, shards(): pl.pallas_call(functools.partial(kernel, Y, Z, B, clusters), out_shape=(j...  88.3 us
    unnamed x6, local copies, waits for them, and re-layouts  3.1 us

profile of v2, /device:TPU:1, one launch (start us, length us, event | category | flops | bytes accessed | tf_op | source)
XLA Modules:
  0.0 92.1 jit_solution(48437682268476455)
XLA Ops:
  0.6 0.0 copy-start.1
  0.6 0.6 copy-done.1
  1.3 0.0 copy-start
  1.3 1.0 %copy-done = f32[128,1024]{1,0:T(8,128)S(1)} copy-done((f32[128,1024]{1,0:T(8,128)S(1)}, f32[128,1024]{1,0:T(8,128)}, u32[]{:S(2)}) %copy-start) | copy-done | bytes 524312
  2.3 88.3 %shard_map.41 = (f32[1,8,8192]{2,1,0:T(8,128)S(1)}, f32[512,128]{1,0:T(8,128)S(1)}) custom-call(f32[128,1024]{1,0:T(8,128)S(1)} %copy-done, s32[1,128]{1,0:T(1,128)S(1)} %bitcast.1), custom_call_target="tpu_custom_call" | custom-call | tf_op jit(solution)/shard_map/pallas_call | solution.py:379
  90.7 0.7 copy.6
  91.4 0.7 copy.7
Async XLA Ops:
  0.6 0.7 copy-start.1
  1.3 1.0 %copy-start = (f32[128,1024]{1,0:T(8,128)S(1)}, f32[128,1024]{1,0:T(8,128)}, u32[]{:S(2)}) copy-start(f32[128,1024]{1,0:T(8,128)} %p_hbm.1) | copy-start | bytes 1572868

commit v3 on v2

v3 whole, which is shorter than its diff:
```python
import functools

import jax
import jax.numpy as jnp
from jax import lax
from jax.experimental import pallas as pl
from jax.experimental.pallas import tpu as pltpu
from jax.sharding import PartitionSpec as P

MESH = pl.DeviceIdType.MESH
EPS = 1e-06
DEPTH = 16
CHUNKS = 4
F32 = jnp.float32
LOW = jnp.bfloat16
NT = (((1,), (1,)), ((), ()))


def iota(shape, dim):
    return lax.broadcasted_iota(jnp.int32, shape, dim)


def kernel(
    Y, Z, B, K, p_hbm, a_hbm, cent_ref, score_ref,
    p_ref, a_ref, docs, own, ids, col, part, got, part0, got0, part_pen, got_pen, part_last, got_last,
    acc, sums, pay_out, pay_in, sq_out, sq_in, nrm, fold_out, fold_in, cent_raw, colscale, pick_last, where_last, hot_last, fold_hot,
    in_sem, zr_send, zr_recv, zl_send, zl_recv, id_send, id_recv, own_send, own_recv,
    rs_send, rs_recv, pay_send, pay_recv, sq_send, sq_recv, nrm_send, nrm_recv,
    f_send, f_recv, u_send, u_recv,
):
    R, W = p_ref.shape
    NP = Z // 2
    LAST = NP
    PLANE = Y * B
    GROUP = K // B
    PART = GROUP // (Y * Z)
    OWN = PART * B
    LANES = PART * Z
    CR = R // CHUNKS
    SUB = R // B
    NC = Y * SUB
    CAP = 8
    HALF = NP // 2
    doc, b = lax.axis_index("doc"), lax.axis_index("bin")
    y, z = doc // Z, doc & (Z - 1)
    me = y * B + b

    def at_z(q):
        return (y * Z + ((z + q) & (Z - 1)), b)

    def at_y(q):
        return (((y + q) & (Y - 1)) * Z + z, b)

    def at_plane(idx):
        return ((idx // B) * Z + z, idx & (B - 1))

    def remote(src, dst, send, recv, device):
        return pltpu.make_async_remote_copy(
            src_ref=src, dst_ref=dst, send_sem=send, recv_sem=recv, device_id=device, device_id_type=MESH
        )

    def wait_bytes(ref, sem):
        pltpu.make_async_copy(ref, ref, sem).wait()

    fetch = pltpu.make_async_copy(p_hbm, p_ref, in_sem.at[0])
    fetch.start()
    fetch_ids = pltpu.make_async_copy(a_hbm, a_ref, in_sem.at[1])
    fetch_ids.start()

    barrier = pltpu.get_barrier_semaphore()

    for q in range(1, HALF + 1):
        for way in (q, -q):
            pl.semaphore_signal(barrier, inc=1, device_id=at_z(way), device_id_type=MESH)

    @pl.loop(1, PLANE)
    def _(q):
        pl.semaphore_signal(barrier, inc=1, device_id=at_plane(((me + q) & (PLANE - 1))), device_id_type=MESH)

    fetch.wait()
    fetch_ids.wait()
    low = p_ref[...].astype(LOW)
    docs[0, 0:R, :] = low
    own[y] = low
    ids[0, :, 0:R] = a_ref[...]
    pl.semaphore_wait(barrier, 2 * HALF + PLANE - 1)

    def right(s, to, row, c):
        return remote(docs.at[s, pl.ds(c * CR, CR)], docs.at[to, pl.ds(row + c * CR, CR)],
                      zr_send.at[s, c], zr_recv.at[to, c], at_z(1))

    def left(s, row, to, c):
        return remote(docs.at[s, pl.ds(row + c * CR, CR)], docs.at[to, pl.ds(R + c * CR, CR)],
                      zl_send.at[s, c], zl_recv.at[to, c], at_z(-1))

    for c in range(CHUNKS):
        right(0, 1, 0, c).start()
        left(0, 0, 1, c).start()
    id_near, id_far = [], []
    for q in range(1, HALF + 1):
        for side, way in ((0, q), (1, -q)):
            k = 2 * q + side
            id_near.append(remote(ids.at[0, :, pl.ds(0, R)], ids.at[q, :, pl.ds(side * R, R)],
                                  id_send.at[k], id_recv.at[k], at_z(way)))
            if q < HALF or side:
                lanes = pl.ds(side * R, R)
                k += 2 * HALF
                id_far.append(remote(ids.at[q, :, lanes], ids.at[(q + HALF) % NP, :, lanes],
                                     id_send.at[k], id_recv.at[k], at_z(-HALF if side else HALF)))
    for copy in id_near:
        copy.start()
    def own_copy(q):
        return remote(docs.at[0, pl.ds(0, R)], own.at[y], own_send.at[q], own_recv.at[q], at_y(q))

    for q in range(1, Y):
        own_copy(q).start()
    acc[...] = jnp.zeros_like(acc)
    sums[...] = jnp.zeros_like(sums)

    def partial(rows, unit, out, into):
        n = rows.shape[0]
        for v in range(Y):
            g = lax.dot_general(own[v], rows, NT, preferred_element_type=F32)
            out[:, v * SUB:(v + 1) * SUB, :] = g.reshape(B, SUB, n).astype(out.dtype)
        for q in range(1, B):
            to = ((b + q) & (B - 1))
            remote(out.at[to], into.at[q - 1], rs_send.at[unit], rs_recv.at[unit], (doc, to)).start()

    def choose(a, column):
        n = a.shape[1]
        a = jnp.broadcast_to(a, (16, n))
        sub = iota((16, n), 0)
        lane = iota((16, n), 1)
        owner = jnp.where(sub < 2 * Y, lax.rem(y + sub // 2, Y) * Z + lax.rem(z + (sub & 1) * NP, Z), -1)
        match = ((a & (GROUP - 1)) // PART) == owner
        local = (a // GROUP) * PART + (a & (PART - 1))
        earlier = (iota((n, n), 0) < iota((n, n), 1)) & (iota((n, n), 0) // R == iota((n, n), 1) // R)
        before = jnp.dot(match.astype(F32).astype(LOW), earlier.astype(F32).astype(LOW), preferred_element_type=F32)
        slot = jnp.where(match, before + CAP * (lane // R).astype(F32), -1.0)
        number = sub.astype(F32)
        if n == R:
            picks = [(number == slot[q:q + 1]) | (number - CAP == slot[q + 1:q + 2]) & (number >= CAP)
                     for q in range(2, 2 * Y, 2)]
        else:
            picks = [number == slot[q:q + 1] for q in range(2, 2 * Y)]
        pick = jnp.concatenate([hit.astype(F32).astype(LOW) for hit in picks], axis=0)
        home = (column // GROUP) * PART + (column & (PART - 1))
        home += jnp.where((((column & (GROUP - 1)) // PART) & (Z - 1)) == z, 0, OWN)
        home = (home == iota((n, 128), 1)).astype(F32).astype(LOW)
        where = jnp.dot(pick, home, preferred_element_type=F32).astype(LOW)
        row = jnp.where(match[0:1], local[0:1], jnp.where(match[1:2], local[1:2] + OWN, -1))
        hot = (iota((2 * OWN, n), 0) == row).astype(F32).astype(LOW)
        return pick, where, hot

    def place(rows, choice, unit):
        pick, where, hot = choice
        picked = jnp.dot(pick, rows, preferred_element_type=F32).astype(LOW)
        tall = pick.shape[0] // (Y - 1)
        for q in range(1, Y):
            out, into = pay_out.at[unit, q - 1, pl.ds(0, tall)], pay_in.at[unit, q - 1, pl.ds(0, tall)]
            out[:, 0:W] = picked[(q - 1) * tall:q * tall]
            out[:, W:W + 128] = where[(q - 1) * tall:q * tall]
            remote(out, into, pay_send.at[unit], pay_recv.at[unit], at_y(q)).start()
        sums[...] += jnp.dot(hot, rows, preferred_element_type=F32)

    def add_placed(unit, tall=32):
        wait_bytes(pay_in.at[unit, :, pl.ds(0, tall)], pay_recv.at[unit])
        for q in range(1, Y):
            d = lax.dot_general(pay_in[unit, q - 1, 0:tall, W:W + 128], pay_in[unit, q - 1, 0:tall, 0:W],
                                (((0,), (0,)), ((), ())), preferred_element_type=F32)
            sums[...] += d[0:2 * OWN]

    def spread(column, g):
        return jnp.concatenate(
            [(column == iota((column.shape[0], 128), 1) + (g * GROUP + t * 128)).astype(F32).astype(LOW)
             for t in range(GROUP // 128)], axis=1)

    def ready(at, column):
        for g in range(B):
            fold_hot[g, at:at + column.shape[0], :] = spread(column, g)

    def finished(out, into):
        h = out[b].astype(F32)
        for i in range(B - 1):
            h += into[i].astype(F32)
        hi = h.astype(LOW)
        lo = (h - hi.astype(F32)).astype(LOW)
        return jnp.concatenate([hi, lo], axis=0)

    def fold(out, into, column, first, count, at=0):
        both = finished(out, into)
        n = both.shape[1]
        for g in range(first, first + count):
            hot = fold_hot[g, at:at + n, :] if column is None else spread(column, g)
            d = jnp.dot(both, hot, preferred_element_type=F32)
            acc[g] += d[0:NC] + d[NC:]

    @pl.loop(1, NP)
    def _(s):
        for c in range(CHUNKS):
            early = c < CHUNKS // 2
            right(0, s, 0, c).wait_recv()
            go = lambda: right(s, ((s + 1) & (NP - 1)), jnp.where(s == NP - 1, R, 0), c).start()
            go() if early else pl.when(s < NP - 1)(go)
            left(0, 0, s, c).wait_recv()
            go_left = lambda: left(s, R, ((s + 1) & (NP - 1)), c).start()
            pl.when(s < NP - 1)(go_left) if early else go_left()

            if c == 0:

                @pl.when(s == 1)
                def _():
                    for copy in id_near:
                        copy.wait()
                    for copy in id_far:
                        copy.start()

                @pl.when(s == 2)
                def _():
                    for copy in id_far:
                        copy.wait()
                    for q in range(1, Y):
                        own_copy(q).wait_send()
                        from_y = lax.rem(y - q + Y, Y)
                        remote(own.at[0], own.at[from_y], own_send.at[q], own_recv.at[q], (doc, b)).wait_recv()

                    @pl.loop(0, NP)
                    def _(p):
                        col[p] = jnp.transpose(jnp.broadcast_to(ids[p, 0:1, :], (128, 2 * R)))

                pl.when(s >= 2)(lambda: partial(docs[s - 1], s - 1, part.at[s - 2], got.at[s - 2]))

            if c == 1:
                pl.when(s >= 2)(lambda: place(docs[s - 1], choose(ids[s - 1], col[s - 1]), s - 1))

                @pl.when(s == 2)
                def _():
                    place(docs[0, 0:R, :], choose(ids[0, :, 0:R], col[0, 0:R, :]), 0)
                    partial(docs[0, 0:R, :], 0, part0, got0)

                @pl.when(s == 3)
                def _():
                    pick_last[...], where_last[...], hot_last[...] = choose(ids[0, :, R:2 * R], col[0, R:2 * R, :])
                    ready(4 * R, col[0, R:2 * R, :])

                pl.when(s == max(3, NP - 4))(lambda: ready(0, col[NP - 2]))
                pl.when(s == max(3, NP - 3))(lambda: ready(2 * R, col[NP - 1]))

                @pl.when(s == max(3, NP - 4))
                def _():
                    wait_bytes(got0, rs_recv.at[0])
                    fold(part0, got0, col[0, 0:R, :], 0, B)
                    add_placed(0, 16)

            if c >= 2:

                @pl.when(s >= 3)
                def _():
                    p = s - 2
                    if c == 2:
                        wait_bytes(got.at[p - 1], rs_recv.at[p])
                    half = B // 2
                    fold(part.at[p - 1], got.at[p - 1], col[p], (c - 2) * half, half)
                    if c == 3:
                        add_placed(p)

    partial(docs[NP - 1], NP - 1, part_pen, got_pen)
    place(docs[NP - 1], choose(ids[NP - 1], col[NP - 1]), NP - 1)
    for c in range(CHUNKS // 2):
        right(0, 0, R, c).wait_recv()
        left(0, 0, 0, c + CHUNKS // 2).wait_recv()
    place(docs[0, R:2 * R, :], (pick_last[...], where_last[...], hot_last[...]), LAST)
    partial(docs[0, R:2 * R, :], LAST, part_last, got_last)
    wait_bytes(got.at[NP - 3], rs_recv.at[NP - 2])
    fold(part.at[NP - 3], got.at[NP - 3], None, 0, B, 0)
    add_placed(NP - 2)
    add_placed(NP - 1)
    wait_bytes(got_pen, rs_recv.at[NP - 1])
    fold(part_pen, got_pen, None, 0, B, 2 * R)
    add_placed(LAST, 16)

    def slab_copy(to):
        return remote(sums.at[pl.ds(pl.multiple_of(to * PART, PART), PART)],
                      cent_raw.at[:, pl.ds(pl.multiple_of(b * W, W), W)], u_send, u_recv, (doc, to))

    square = jnp.sum(sums[...] * sums[...], axis=1, keepdims=True)
    square = jnp.broadcast_to(square, (2 * OWN, 128))
    if 2 * OWN < 128:
        square = jnp.concatenate([square, jnp.zeros((128 - 2 * OWN, 128), F32)], axis=0)
    sq_out[...] = jnp.transpose(square)[0:1]

    @pl.loop(1, PLANE)
    def _(q):
        idx = ((me + q) & (PLANE - 1))
        remote(sq_out, sq_in.at[PLANE - 1 - q], sq_send, sq_recv, at_plane(idx)).start()

    wait_bytes(got_last, rs_recv.at[LAST])
    both = finished(part_last, got_last)

    def fold_piece(v, g):
        return fold_out.at[g, pl.ds(pl.multiple_of(v * SUB, SUB), SUB)], fold_in.at[me]

    for i in range(B):
        g = (b + 1 + i) & (B - 1)
        d = jnp.dot(both, fold_hot[g, 4 * R:5 * R, :], preferred_element_type=F32)
        fold_out[g] = (acc[g] + d[0:NC] + d[NC:]).astype(LOW)
        for j in range(Y):
            v = (y + j) & (Y - 1)
            src, dst = fold_piece(v, g)
            if i == B - 1 and j == 0:
                pltpu.make_async_copy(src, dst, f_recv).start()
            else:
                remote(src, dst, f_send, f_recv, (v * Z + z, g)).start()

    wait_bytes(sq_in, sq_recv)
    sub = iota((8, 128), 0)
    lane = iota((8, 128), 1)
    table = jnp.zeros((8, 128), F32)
    for i in range(PLANE):
        row = sq_out[...] if i == PLANE - 1 else sq_in[i]
        v = ((me + i + 1) & (PLANE - 1)) // B
        table += jnp.where(sub == v, row, 0.0)
    inverse = lax.rsqrt(table + EPS)
    far = lax.rem(z + NP, Z)
    near = pltpu.roll(inverse, lax.rem((z - b) * PART + 128, 128), 1)
    turned = jnp.where((lane >= z * PART) & (lane < (z + 1) * PART), near, 0.0)
    beyond = pltpu.roll(inverse, lax.rem((far - b) * PART - OWN + 256, 128), 1)
    turned += jnp.where((lane >= far * PART) & (lane < (far + 1) * PART), beyond, 0.0)
    nrm[NP - 1] = turned[0:Y]
    reach = [q for q in range(1 - NP // 2, NP // 2 + 1) if q]
    for i, q in enumerate(reach):
        remote(nrm.at[NP - 1], nrm.at[i], nrm_send, nrm_recv, at_z(q)).start()

    for q in range(1, B):
        slab_copy(((b + q) & (B - 1))).start()
    cent_raw[:, pl.ds(pl.multiple_of(b * W, W), W)] = sums[pl.ds(pl.multiple_of(b * PART, PART), PART), :]


    ours = jnp.sum(jnp.where(sub == y, inverse, 0.0), axis=0, keepdims=True)
    colscale[...] = jnp.transpose(jnp.broadcast_to(ours, (128, 128)))
    scale = colscale[pl.ds(pl.multiple_of(b * PART, PART), PART), :]
    wait_bytes(cent_raw.at[:, pl.ds(0, (B - 1) * W)], u_recv)
    for t in range(B * W // 128):
        cent_ref[0, :, t * 128:(t + 1) * 128] = cent_raw[:, t * 128:(t + 1) * 128] * scale

    wait_bytes(fold_in, f_recv)
    raw = fold_in[0:B].astype(F32)
    for v in range(1, Y):
        raw += fold_in[v * B:(v + 1) * B].astype(F32)
    raw = raw.reshape(R, GROUP)
    wait_bytes(nrm.at[pl.ds(0, NP - 1)], nrm_recv)
    rows = nrm[0]
    for i in range(1, NP):
        rows += nrm[i]
    for v in range(Y):
        tile = raw[:, v * LANES:(v + 1) * LANES] * rows[v:v + 1, :]
        score_ref[v * LANES:(v + 1) * LANES, :] = jnp.transpose(tile)

    @pl.loop(0, NP)
    def _(s):
        for c in range(CHUNKS):
            early = c < CHUNKS // 2
            wait_right = lambda: right(s, s, 0, c).wait_send()
            wait_left = lambda: left(s, 0, s, c).wait_send()
            wait_right() if early else pl.when(s < NP - 1)(wait_right)
            pl.when(s < NP - 1)(wait_left) if early else wait_left()

    for p in range(NP - 2):
        wait_bytes(got.at[p], rs_send.at[p + 1])
    wait_bytes(got0, rs_send.at[0])
    wait_bytes(got_pen, rs_send.at[NP - 1])
    wait_bytes(got_last, rs_send.at[LAST])
    for u in range(NP + 1):
        wait_bytes(pay_in.at[u, :, pl.ds(0, 16 if u in (0, LAST) else 32)], pay_send.at[u])
    wait_bytes(fold_in.at[pl.ds(0, PLANE - 1)], f_send)
    wait_bytes(sq_in, sq_send)
    wait_bytes(nrm.at[pl.ds(0, NP - 1)], nrm_send)
    wait_bytes(cent_raw.at[:, pl.ds(0, (B - 1) * W)], u_send)


def program(mesh, Z, clusters):
    B = mesh.shape["bin"]
    Y = mesh.shape["doc"] // Z
    NP = Z // 2

    def shards(profiles, assign):
        R, W = profiles.shape
        group = clusters // B
        part = group // (Y * Z)
        own = part * B
        SUB = R // B
        NC = Y * SUB
        plane = Y * B
        dma = pltpu.SemaphoreType.DMA
        scratch = [
            pltpu.VMEM((R, W), F32),
            pltpu.VMEM((1, R), jnp.int32),
            pltpu.VMEM((NP, 2 * R, W), LOW),
            pltpu.VMEM((Y, R, W), LOW),
            pltpu.VMEM((NP, 1, 2 * R), jnp.int32),
            pltpu.VMEM((NP, 2 * R, 128), jnp.int32),
            pltpu.VMEM((NP - 2, B, NC, 2 * R), LOW),
            pltpu.VMEM((NP - 2, B - 1, NC, 2 * R), LOW),
            pltpu.VMEM((B, NC, R), LOW),
            pltpu.VMEM((B - 1, NC, R), LOW),
            pltpu.VMEM((B, NC, 2 * R), LOW),
            pltpu.VMEM((B - 1, NC, 2 * R), LOW),
            pltpu.VMEM((B, NC, R), LOW),
            pltpu.VMEM((B - 1, NC, R), LOW),
            pltpu.VMEM((B, NC, group), F32),
            pltpu.VMEM((2 * own, W), F32),
            pltpu.VMEM((NP + 1, Y - 1, 32, W + 128), LOW),
            pltpu.VMEM((NP + 1, Y - 1, 32, W + 128), LOW),
            pltpu.VMEM((1, 128), F32),
            pltpu.VMEM((plane - 1, 1, 128), F32),
            pltpu.VMEM((NP, Y, 128), F32),
            pltpu.VMEM((B, NC, group), LOW),
            pltpu.VMEM((plane, SUB, group), LOW),
            pltpu.VMEM((part, B * W), F32),
            pltpu.VMEM((128, 128), F32),
            pltpu.VMEM(((Y - 1) * 16, R), LOW),
            pltpu.VMEM(((Y - 1) * 16, 128), LOW),
            pltpu.VMEM((2 * own, R), LOW),
            pltpu.VMEM((B, 5 * R, group), LOW),
            dma((2,)),
            *[dma((NP, CHUNKS))] * 4,
            *[dma((Z + 2,))] * 2,
            *[dma((Y,))] * 2,
            *[dma((NP + 1,))] * 4,
            *[dma] * 8,
        ]
        return pl.pallas_call(
            functools.partial(kernel, Y, Z, B, clusters),
            out_shape=(
                jax.ShapeDtypeStruct((1, part, B * W), F32),
                jax.ShapeDtypeStruct((group, R), F32),
            ),
            in_specs=[pl.BlockSpec(memory_space=pltpu.HBM)] * 2,
            out_specs=(pl.BlockSpec(memory_space=pltpu.VMEM),) * 2,
            scratch_shapes=scratch,
            compiler_params=pltpu.CompilerParams(
                collective_id=0, has_side_effects=True, vmem_limit_bytes=60 * 2**20
            ),
        )(profiles, assign.reshape(1, -1))

    return jax.shard_map(
        shards,
        mesh=mesh,
        in_specs=(P("doc", "bin"), P("doc")),
        out_specs=(P("bin", "doc", None), P("bin", "doc")),
        check_vma=False,
    )


def solution(mesh):
    return program(mesh, DEPTH, 4096)
```

time: 92.2 us -> 87.1 us (0.945)
  Pallas kernels: 88.3 us -> 83.9 us
    pallas_call x1, Pallas kernels: 88.3 us -> 83.9 us  [shards(): pl.pallas_call(functools.partial(kernel, Y, Z, B, clusters), out_shape=(j...]
    unnamed x6 -> x4, local copies, waits for them, and re-layouts: 3.1 us -> 2.42 us
where the time goes in v3:
time: 87.1 us; the launch traced here: 87 us
  Pallas kernels  83.9 us (96%)
  local copies, waits for them, and re-layouts  2.42 us (3%)
    pallas_call x1, Pallas kernels, shards(): pl.pallas_call(functools.partial(kernel, Y, Z, B, clusters), out_shape=(j...  83.9 us
    unnamed x4, local copies, waits for them, and re-layouts  2.42 us

profile of v3, /device:TPU:1, one launch (start us, length us, event | category | flops | bytes accessed | tf_op | source)
XLA Modules:
  0.0 87.0 jit_solution(8870242091485002341)
XLA Ops:
  0.6 83.9 %shard_map.41 = (f32[1,8,8192]{2,1,0:T(8,128)}, f32[512,128]{1,0:T(8,128)}) custom-call(f32[128,1024]{1,0:T(8,128)} %p_hbm.1, s32[1,128]{1,0:T(1,128)} %bitcast.1), custom_call_target="tpu_custom_call" | custom-call | tf_op jit(solution)/shard_map/pallas_call | solution.py:432
  84.6 0.0 copy-start
  84.6 1.7 %copy.6 = f32[1,8,8192]{2,1,0:T(8,128)} copy(f32[1,8,8192]{2,1,0:T(8,128)} %get-tuple-element.4) | data formatting | bytes 524288
  86.3 0.0 copy-done
  86.3 0.7 copy.7
Async XLA Ops:
  84.6 1.7 %copy-start = (f32[512,128]{1,0:T(8,128)S(1)}, f32[512,128]{1,0:T(8,128)}, u32[]{:S(2)}) copy-start(f32[512,128]{1,0:T(8,128)} %get-tuple-element.5) | copy-start | bytes 786436

commit v4 on v3

--- a/solution.py
+++ b/solution.py
@@ -195,6 +195,9 @@
             d = jnp.dot(both, hot, preferred_element_type=F32)
             acc[g] += d[0:NC] + d[NC:]
 
+    def column(p):
+        return jnp.transpose(jnp.broadcast_to(ids[p], (128, 2 * R)))
+
     @pl.loop(1, NP)
     def _(s):
         for c in range(CHUNKS):
@@ -219,37 +222,42 @@
                 def _():
                     for copy in id_far:
                         copy.wait()
+
+                @pl.when(s >= 2)
+                def _():
+                    col[s - 1] = column(s - 1)
+                    place(docs[s - 1], choose(ids[s - 1], col[s - 1]), s - 1)
+
+                @pl.when(s == 3)
+                def _():
+                    place(docs[0, 0:R, :], choose(ids[0, :, 0:R], column(0)[0:R]), 0)
+
+            if c == 1:
+
+                @pl.when(s == 2)
+                def _():
                     for q in range(1, Y):
                         own_copy(q).wait_send()
-                        from_y = lax.rem(y - q + Y, Y)
+                        from_y = (y - q) & (Y - 1)
                         remote(own.at[0], own.at[from_y], own_send.at[q], own_recv.at[q], (doc, b)).wait_recv()
 
-                    @pl.loop(0, NP)
-                    def _(p):
-                        col[p] = jnp.transpose(jnp.broadcast_to(ids[p, 0:1, :], (128, 2 * R)))
-
                 pl.when(s >= 2)(lambda: partial(docs[s - 1], s - 1, part.at[s - 2], got.at[s - 2]))
-
-            if c == 1:
-                pl.when(s >= 2)(lambda: place(docs[s - 1], choose(ids[s - 1], col[s - 1]), s - 1))
-
-                @pl.when(s == 2)
-                def _():
-                    place(docs[0, 0:R, :], choose(ids[0, :, 0:R], col[0, 0:R, :]), 0)
-                    partial(docs[0, 0:R, :], 0, part0, got0)
-
-                @pl.when(s == 3)
-                def _():
-                    pick_last[...], where_last[...], hot_last[...] = choose(ids[0, :, R:2 * R], col[0, R:2 * R, :])
-                    ready(4 * R, col[0, R:2 * R, :])
-
-                pl.when(s == max(3, NP - 4))(lambda: ready(0, col[NP - 2]))
-                pl.when(s == max(3, NP - 3))(lambda: ready(2 * R, col[NP - 1]))
+                pl.when(s == 3)(lambda: partial(docs[0, 0:R, :], 0, part0, got0))
+                pl.when(s == max(3, NP - 4))(lambda: ready(0, column(NP - 2)))
+                pl.when(s == max(3, NP - 2))(lambda: ready(2 * R, column(NP - 1)))
+
+                @pl.when(s == max(3, NP - 3))
+                def _():
+                    last = column(0)[R:2 * R]
+                    pick_last[...], where_last[...], hot_last[...] = choose(ids[0, :, R:2 * R], last)
+                    ready(4 * R, last)
+
+            if c == 2:
 
                 @pl.when(s == max(3, NP - 4))
                 def _():
                     wait_bytes(got0, rs_recv.at[0])
-                    fold(part0, got0, col[0, 0:R, :], 0, B)
+                    fold(part0, got0, column(0)[0:R], 0, B)
                     add_placed(0, 16)
 
             if c >= 2:
@@ -265,7 +273,7 @@
                         add_placed(p)
 
     partial(docs[NP - 1], NP - 1, part_pen, got_pen)
-    place(docs[NP - 1], choose(ids[NP - 1], col[NP - 1]), NP - 1)
+    place(docs[NP - 1], choose(ids[NP - 1], column(NP - 1)), NP - 1)
     for c in range(CHUNKS // 2):
         right(0, 0, R, c).wait_recv()
         left(0, 0, 0, c + CHUNKS // 2).wait_recv()
@@ -432,8 +440,8 @@
         return pl.pallas_call(
             functools.partial(kernel, Y, Z, B, clusters),
             out_shape=(
-                jax.ShapeDtypeStruct((1, part, B * W), F32),
-                jax.ShapeDtypeStruct((group, R), F32),
+                pltpu.VMEM((1, part, B * W), F32),
+                pltpu.VMEM((group, R), F32),
             ),
             in_specs=[pl.BlockSpec(memory_space=pltpu.HBM)] * 2,
             out_specs=(pl.BlockSpec(memory_space=pltpu.VMEM),) * 2,

time: 87.1 us -> 84.7 us (0.972)
  Pallas kernels: 83.9 us -> 82.5 us
  local copies, waits for them, and re-layouts: 2.42 us -> 1.41 us
    pallas_call x1, Pallas kernels: 83.9 us -> 82.5 us  [shards(): pl.pallas_call(functools.partial(kernel, Y, Z, B, clusters), out_shape=(p...]
    unnamed x4 -> x2, local copies, waits for them, and re-layouts: 2.42 us -> 1.41 us
where the time goes in v4:
time: 84.7 us; the launch traced here: 84.6 us
  Pallas kernels  82.5 us (97%)
  local copies, waits for them, and re-layouts  1.41 us (2%)
    pallas_call x1, Pallas kernels, shards(): pl.pallas_call(functools.partial(kernel, Y, Z, B, clusters), out_shape=(p...  82.5 us

profile of v4, /device:TPU:1, one launch (start us, length us, event | category | flops | bytes accessed | tf_op | source)
XLA Modules:
  0.0 84.6 jit_solution(15785430271653392233)
XLA Ops:
  0.6 82.5 %shard_map.41 = (f32[1,8,8192]{2,1,0:T(8,128)S(1)}, f32[512,128]{1,0:T(8,128)S(1)}) custom-call(f32[128,1024]{1,0:T(8,128)} %p_hbm.1, s32[1,128]{1,0:T(1,128)} %bitcast.1), custom_call_target="tpu_custom_call" | custom-call | tf_op jit(solution)/shard_map/pallas_call | solution.py:440
  83.2 0.7 copy.6
  83.9 0.7 copy.7

commit v5 on v4

--- a/solution.py
+++ b/solution.py
@@ -344,6 +344,23 @@
     cent_raw[:, pl.ds(pl.multiple_of(b * W, W), W)] = sums[pl.ds(pl.multiple_of(b * PART, PART), PART), :]
 
 
+    @pl.loop(0, NP)
+    def _(s):
+        for c in range(CHUNKS):
+            early = c < CHUNKS // 2
+            wait_right = lambda: right(s, s, 0, c).wait_send()
+            wait_left = lambda: left(s, 0, s, c).wait_send()
+            wait_right() if early else pl.when(s < NP - 1)(wait_right)
+            pl.when(s < NP - 1)(wait_left) if early else wait_left()
+
+    for p in range(NP - 2):
+        wait_bytes(got.at[p], rs_send.at[p + 1])
+    wait_bytes(got0, rs_send.at[0])
+    wait_bytes(got_pen, rs_send.at[NP - 1])
+    wait_bytes(got_last, rs_send.at[LAST])
+    for u in range(NP + 1):
+        wait_bytes(pay_in.at[u, :, pl.ds(0, 16 if u in (0, LAST) else 32)], pay_send.at[u])
+
     ours = jnp.sum(jnp.where(sub == y, inverse, 0.0), axis=0, keepdims=True)
     colscale[...] = jnp.transpose(jnp.broadcast_to(ours, (128, 128)))
     scale = colscale[pl.ds(pl.multiple_of(b * PART, PART), PART), :]
@@ -364,22 +381,6 @@
         tile = raw[:, v * LANES:(v + 1) * LANES] * rows[v:v + 1, :]
         score_ref[v * LANES:(v + 1) * LANES, :] = jnp.transpose(tile)
 
-    @pl.loop(0, NP)
-    def _(s):
-        for c in range(CHUNKS):
-            early = c < CHUNKS // 2
-            wait_right = lambda: right(s, s, 0, c).wait_send()
-            wait_left = lambda: left(s, 0, s, c).wait_send()
-            wait_right() if early else pl.when(s < NP - 1)(wait_right)
-            pl.when(s < NP - 1)(wait_left) if early else wait_left()
-
-    for p in range(NP - 2):
-        wait_bytes(got.at[p], rs_send.at[p + 1])
-    wait_bytes(got0, rs_send.at[0])
-    wait_bytes(got_pen, rs_send.at[NP - 1])
-    wait_bytes(got_last, rs_send.at[LAST])
-    for u in range(NP + 1):
-        wait_bytes(pay_in.at[u, :, pl.ds(0, 16 if u in (0, LAST) else 32)], pay_send.at[u])
     wait_bytes(fold_in.at[pl.ds(0, PLANE - 1)], f_send)
     wait_bytes(sq_in, sq_send)
     wait_bytes(nrm.at[pl.ds(0, NP - 1)], nrm_send)

time: 84.7 us -> 84.6 us (level)
  no operation moved by 1% of the time
where the time goes in v5:
time: 84.6 us; the launch traced here: 84.4 us
  Pallas kernels  82.4 us (97%)
  local copies, waits for them, and re-layouts  1.41 us (2%)
    pallas_call x1, Pallas kernels, shards(): pl.pallas_call(functools.partial(kernel, Y, Z, B, clusters), out_shape=(p...  82.4 us

profile of v5, /device:TPU:1, one launch (start us, length us, event | category | flops | bytes accessed | tf_op | source)
XLA Modules:
  0.0 84.4 jit_solution(2355100325269468759)
XLA Ops:
  0.6 82.4 %shard_map.41 = (f32[1,8,8192]{2,1,0:T(8,128)S(1)}, f32[512,128]{1,0:T(8,128)S(1)}) custom-call(f32[128,1024]{1,0:T(8,128)} %p_hbm.1, s32[1,128]{1,0:T(1,128)} %bitcast.1), custom_call_target="tpu_custom_call" | custom-call | tf_op jit(solution)/shard_map/pallas_call | solution.py:441
  83.0 0.7 copy.6
  83.7 0.7 copy.7
